TPU v7x, 256 devices: a whole 4x4x8 slice. The times are simulated.
256 devices in a mesh: row: 16 (over y_hi, z), col: 16 (over y_lo, x, core).
Axes of the slice: x: 4, y: 4 (y_hi: 2, y_lo: 2; y = y_hi * 2 + y_lo), z: 8, core: 2. Of those that a mesh axis runs over, the one named last changes fastest.
Arguments:
- start_rows: int32 [4], replicated, may hold values from 0 to 13, as said below
- initial: bfloat16 [4, 16, 256, 8, 256], P(None, 'col'), may hold values from -6 to 6
- site_tensors: bfloat16 [16, 16, 4096], P('row', 'col'), may hold values from -4 to 4
- charges: int32 [16, 16, 4, 8], P('row', 'col'), may hold values from 0 to 2
- right_proj: bfloat16 [16, 16, 256, 8, 256], P('row', 'col'), may hold values from -0.125 to 0.125
- left_proj: bfloat16 [16, 16, 256, 8, 256], P('row', 'col'), may hold values from -0.125 to 0.125
- kept_ranks: int32 [16, 16], P('row', 'col'), may hold values from 128 to 256
Outputs:
- absorbed: bfloat16 [16, 16, 256, 8, 256], P('row', 'col')
Inputs may be any that keep to these rules, and one draw needn't show every extreme that they name: `start_rows`: the start rows are distinct; one is 0 and one is 13.
All inputs are finite; a program needn't handle non-finite values.
Results may differ from a plain program's by a relative error of at most 0.02.
Values may be sent and summed in bfloat16 or wider, within the bound.
A program may use at most 64 MiB of HBM per device.

v0:
```python
import functools

import jax
import jax.numpy as jnp
from jax import lax
from jax.experimental import pallas as pl
from jax.experimental.pallas import tpu as pltpu
from jax.sharding import PartitionSpec as P

ABSORB = 3
CHUNKS = 8
MESH = pl.DeviceIdType.MESH
BF16 = jnp.bfloat16
F32 = jnp.float32


def dot(a, b):
    return lax.dot_general(a, b, (((1,), (0,)), ((), ())), preferred_element_type=F32)


def dot_t(a, b):
    return lax.dot_general(a, b, (((1,), (1,)), ((), ())), preferred_element_type=F32)


def iota(shape, dim):
    return lax.broadcasted_iota(jnp.int32, shape, dim)


def block_operator(tensor_ref, charges_ref, inner, group):
    wide = inner * inner * inner
    row = iota((inner, wide), 0)
    col = iota((inner, wide), 1)
    up, down, right = col // (inner * inner), (col // inner) % inner, col % inner
    flat = tensor_ref[...].astype(F32)
    value = jnp.zeros((inner, wide), F32)
    total = jnp.zeros((inner, wide), jnp.int32)
    for v in range(inner):
        value = jnp.where(row == v, flat[:, v * wide : (v + 1) * wide], value)
        total = total + jnp.where(row == v, charges_ref[0, v], 0)
        total = total + jnp.where(up == v, charges_ref[1, v], 0)
        total = total - jnp.where(down == v, charges_ref[2, v], 0)
        total = total - jnp.where(right == v, charges_ref[3, v], 0)
    total = total + 6
    value = jnp.where(total % 3 == 0, value, 0.0)
    block = inner * group
    full = inner * block
    tiled = jnp.concatenate([value] * (full // inner), axis=0)
    down_of_row = iota((full, wide), 0) // block
    down_of_col = (iota((full, wide), 1) // inner) % inner
    tiled = jnp.where(down_of_row == down_of_col, tiled, 0.0).astype(BF16)
    src, dst = iota((wide, full), 0), iota((wide, full), 1)
    same_up = src // (inner * inner) == dst % inner
    same_right = src % inner == dst // block
    pick = jnp.where(same_up & same_right, 1.0, 0.0).astype(BF16)
    spread = dot(tiled, pick)
    a_row = (iota((full, full), 0) // inner) % group
    a_col = (iota((full, full), 1) // inner) % group
    return jnp.where(a_row == a_col, spread, 0.0)


def kernel(
    outer,
    inner,
    envs,
    start_ref,
    kept_ref,
    charges_ref,
    tensor_ref,
    initial_hbm,
    right_hbm,
    left_hbm,
    out_hbm,
    initial_v,
    raw,
    right_v,
    left_own,
    left_in,
    half,
    sites,
    acc,
    operator,
    outgoing,
    arrived,
    load_sem,
    left_send,
    left_recv,
    send_sem,
    recv_sem,
    store_sem,
):
    rows, cols = lax.axis_size("row"), lax.axis_size("col")
    row, col = lax.axis_index("row"), lax.axis_index("col")
    right_col = lax.rem(col + 1, cols)
    left_col = lax.rem(col + cols - 1, cols)
    size = outer * inner
    part = size // CHUNKS
    keys = outer // CHUNKS
    full = outer
    group = full // (inner * inner)
    groups = keys // group
    block = group * inner
    has_next = row < rows - 1
    has_before = row > 0

    load_left = pltpu.make_async_copy(left_hbm, raw.at[0], load_sem.at[0])
    load_right = pltpu.make_async_copy(right_hbm, raw.at[1], load_sem.at[1])
    load_initial = pltpu.make_async_copy(initial_hbm, initial_v, load_sem.at[2])
    load_left.start()
    load_right.start()
    load_initial.start()

    barrier = pltpu.get_barrier_semaphore()
    pl.semaphore_signal(barrier, inc=1, device_id=(row, right_col), device_id_type=MESH)
    pl.semaphore_signal(barrier, inc=1, device_id=(row, left_col), device_id_type=MESH)

    @pl.when(has_next)
    def _():
        pl.semaphore_signal(barrier, inc=1, device_id=(row + 1, col), device_id_type=MESH)

    @pl.when(has_before)
    def _():
        pl.semaphore_signal(barrier, inc=1, device_id=(row - 1, col), device_id_type=MESH)

    kept = kept_ref[0, 0]

    load_left.wait()
    kk = iota((full, full), 0)
    keep_eye = jnp.where((kk == iota((full, full), 1)) & (kk < kept), 1.0, 0.0).astype(BF16)
    for i in range(CHUNKS):
        left_own[i] = dot_t(keep_eye, raw[0, i * part : (i + 1) * part, :]).astype(BF16)

    pl.semaphore_wait(barrier, 2 + jnp.where(has_next, 1, 0) + jnp.where(has_before, 1, 0))

    def left_copy(i):
        span = pl.ds(i * keys, keys)
        return pltpu.make_async_remote_copy(
            src_ref=left_own.at[:, span, :],
            dst_ref=left_in.at[:, span, :],
            send_sem=left_send.at[i],
            recv_sem=left_recv.at[i],
            device_id=(row, right_col),
            device_id_type=MESH,
        )

    for i in range(CHUNKS):
        left_copy(i).start()

    def boundary_copy(step, i):
        span = pl.ds(i * part, part)
        return pltpu.make_async_remote_copy(
            src_ref=outgoing.at[step, span, :],
            dst_ref=arrived.at[step, span, :],
            send_sem=send_sem.at[step, i],
            recv_sem=recv_sem.at[step, i],
            device_id=(row + 1, col),
            device_id_type=MESH,
        )

    load_right.wait()
    to = iota((full, full), 0)
    frm = iota((full, full), 1)
    split = jnp.where(frm == (to % keys) * inner + to // keys, 1.0, 0.0).astype(BF16)
    merge = jnp.where(frm == (to % inner) * keys + to // inner, 1.0, 0.0).astype(BF16)
    inside = iota((full, full), 1) < kept
    for i in range(CHUNKS):
        moved = dot(split, raw[1, i * part : (i + 1) * part, :])
        moved = jnp.where(inside, moved, 0.0).astype(BF16)
        right_v[:, i * keys : (i + 1) * keys, :] = moved.reshape(inner, keys, full)

    operator[...] = block_operator(tensor_ref, charges_ref, inner, group).astype(BF16)

    @pl.when(jnp.logical_not(has_before))
    def _():
        arrived[...] = jnp.zeros_like(arrived)

    def absorb_sites(x, op_ref, i):
        for s in range(inner):
            half[s] = dot(x, right_v[s]).astype(BF16)
        for g in range(groups):
            piece = half[:, g * block : (g + 1) * block, :].reshape(full, full)
            made = dot(op_ref[...], piece).astype(BF16).reshape(inner, block, full)
            sites[:, pl.ds(i * part + g * block, block), :] = made

    load_initial.wait()

    def first(i, carry):
        x = jnp.zeros((part, outer), F32)
        for e in range(envs):
            here = jnp.full((part, outer), start_ref[e], jnp.int32) == row
            span = pl.ds(pl.multiple_of(e * size + i * part, part), part)
            x = jnp.where(here, initial_v[span, :].astype(F32), x)
        absorb_sites(x.astype(BF16), operator, i)
        return carry

    lax.fori_loop(0, CHUNKS, first, 0)

    def first_out(i, carry):
        left_copy(i).wait_recv()
        span = pl.ds(i * keys, keys)
        made = []
        for d in range(inner):
            total = dot(left_in[0, span, :], sites[d, 0:part, :])
            for c in range(1, CHUNKS):
                total += dot(left_in[c, span, :], sites[d, c * part : (c + 1) * part, :])
            made.append(total.astype(BF16))
        stacked = jnp.concatenate(made, axis=0)
        outgoing[0, pl.ds(i * part, part), :] = dot(merge, stacked).astype(BF16)

        @pl.when(has_next)
        def _():
            boundary_copy(0, i).start()

        return carry

    lax.fori_loop(0, CHUNKS, first_out, 0)

    for step in range(1, ABSORB):
        acc[...] = jnp.zeros_like(acc)

        def take(i, carry, step=step):
            @pl.when(has_before)
            def _():
                boundary_copy(step - 1, i).wait_recv()

            span = pl.ds(pl.multiple_of(i * part, part), part)
            absorb_sites(arrived[step - 1, span, :], operator, i)
            for d in range(inner):
                acc[d] += dot(left_in[i], sites[d, span, :])
            return carry

        lax.fori_loop(0, CHUNKS, take, 0)

        def give(i, carry, step=step):
            span = pl.ds(pl.multiple_of(i * keys, keys), keys)
            stacked = acc[:, span, :].astype(BF16).reshape(full, full)
            at = pl.ds(pl.multiple_of(i * part, part), part)
            outgoing[step, at, :] = dot(merge, stacked).astype(BF16)
            if step < ABSORB - 1:

                @pl.when(has_next)
                def _():
                    boundary_copy(step, i).start()

            else:
                pltpu.make_async_copy(outgoing.at[step, at, :], out_hbm.at[at, :], store_sem.at[i]).start()
            return carry

        lax.fori_loop(0, CHUNKS, give, 0)

    def finish(i, carry):
        left_copy(i).wait_send()

        @pl.when(has_next)
        def _():
            for step in range(ABSORB - 1):
                boundary_copy(step, i).wait_send()

        at = pl.ds(pl.multiple_of(i * part, part), part)
        pltpu.make_async_copy(outgoing.at[ABSORB - 1, at, :], out_hbm.at[at, :], store_sem.at[i]).wait()
        return carry

    lax.fori_loop(0, CHUNKS, finish, 0)


def shards(start_rows, initial, site_tensors, charges, right_proj, left_proj, kept_ranks):
    envs, _, outer, inner, _ = initial.shape
    size = outer * inner
    smem = pl.BlockSpec(memory_space=pltpu.SMEM)
    vmem = pl.BlockSpec(memory_space=pltpu.VMEM)
    hbm = pl.BlockSpec(memory_space=pl.ANY)
    out = pl.pallas_call(
        functools.partial(kernel, outer, inner, envs),
        out_shape=jax.ShapeDtypeStruct((size, outer), BF16),
        in_specs=[smem, smem, smem, vmem, hbm, hbm, hbm],
        out_specs=hbm,
        scratch_shapes=[
            pltpu.VMEM((envs * size, outer), BF16),
            pltpu.VMEM((2, size, outer), BF16),
            pltpu.VMEM((inner, outer, outer), BF16),
            pltpu.VMEM((CHUNKS, outer, size // CHUNKS), BF16),
            pltpu.VMEM((CHUNKS, outer, size // CHUNKS), BF16),
            pltpu.VMEM((inner, size // CHUNKS, outer), BF16),
            pltpu.VMEM((inner, size, outer), BF16),
            pltpu.VMEM((inner, outer, outer), F32),
            pltpu.VMEM((outer, outer), BF16),
            pltpu.VMEM((ABSORB, size, outer), BF16),
            pltpu.VMEM((ABSORB - 1, size, outer), BF16),
            pltpu.SemaphoreType.DMA((3,)),
            pltpu.SemaphoreType.DMA((CHUNKS,)),
            pltpu.SemaphoreType.DMA((CHUNKS,)),
            pltpu.SemaphoreType.DMA((ABSORB - 1, CHUNKS)),
            pltpu.SemaphoreType.DMA((ABSORB - 1, CHUNKS)),
            pltpu.SemaphoreType.DMA((CHUNKS,)),
        ],
        compiler_params=pltpu.CompilerParams(
            collective_id=0, has_side_effects=True, vmem_limit_bytes=56 * 1024 * 1024
        ),
        cost_estimate=pl.CostEstimate(
            flops=ABSORB * 6 * size * size * outer, bytes_accessed=8 * size * outer * 2, transcendentals=0
        ),
    )(
        start_rows,
        kept_ranks,
        charges[0, 0],
        site_tensors[0],
        initial.reshape(envs * size, outer),
        right_proj.reshape(size, outer),
        left_proj.reshape(size, outer),
    )
    return out.reshape(1, 1, outer, inner, outer)


def solution(mesh):
    return jax.shard_map(
        shards,
        mesh=mesh,
        in_specs=(
            P(),
            P(None, "col", None, None, None),
            P("row", "col", None),
            P("row", "col", None, None),
            P("row", "col", None, None, None),
            P("row", "col", None, None, None),
            P("row", "col"),
        ),
        out_specs=P("row", "col", None, None, None),
        check_vma=False,
    )
```

profile of v0, /device:TPU:16, one launch (start us, length us, event | category | flops | bytes accessed | tf_op | source)
XLA Modules:
  0.0 72.3 jit_solution(10536714014379584262)
XLA Ops:
  0.7 69.4 %shard_map.73 = bf16[2048,256]{1,0:T(8,128)(2,1)} custom-call(s32[4]{0:T(128)} %start_ref.1, s32[1,1]{1,0:T(1,128)S(6)} %copy.9.kept_ref, s32[4,8]{1,0:T(4,128)} %bitcast.11, bf16[1,4096]{1,0:T(2,128)(2,1)} %bitcast.10, bf16[8192,256]{1,0:T(8,128)(2,1)} %bitcast.7, bf16[2048,256]{1,0:T(8,128)(2,1)} %bitcast.8, bf16[2048,256]{1,0:T(8,128)(2,1)} %bitcast.9), custom_call_target="tpu_custom_call" | custom-call | flops 19327352832 | bytes 8388608 | tf_op jit(solution)/shard_map/pallas_call | solution.py:271
  70.0 2.3 %copy.10 = bf16[1,1,256,8,256]{4,3,2,1,0:T(8,128)(2,1)} copy(bf16[1,1,256,8,256]{4,3,2,1,0:T(8,128)(2,1)} %bitcast.6) | data formatting | bytes 2097152
where the time goes:
time: 73.7 us; the launch traced here: 72.3 us
  Pallas kernels  69.4 us (94%)
  local copies, waits for them, and re-layouts  2.26 us (3%)
    pallas_call x1, Pallas kernels, shards(): pl.pallas_call(functools.partial(kernel, outer, inner, envs), out_shape=j...  69.4 us
    unnamed x1, local copies, waits for them, and re-layouts  2.26 us

commit v1 on v0

v1 whole, which is shorter than its diff:
```python
import functools

import jax
import jax.numpy as jnp
from jax import lax
from jax.experimental import pallas as pl
from jax.experimental.pallas import tpu as pltpu
from jax.sharding import PartitionSpec as P

ABSORB = 3
CHUNKS = 8
LEFT_PARTS = 4
MESH = pl.DeviceIdType.MESH
BF16 = jnp.bfloat16
F32 = jnp.float32


def dot(a, b):
    return lax.dot_general(a, b, (((1,), (0,)), ((), ())), preferred_element_type=F32)


def dot_t(a, b):
    return lax.dot_general(a, b, (((1,), (1,)), ((), ())), preferred_element_type=F32)


def iota(shape, dim):
    return lax.broadcasted_iota(jnp.int32, shape, dim)


def block_operator(tensor_ref, charges_ref, inner, group):
    wide = inner * inner * inner
    row = iota((inner, wide), 0)
    col = iota((inner, wide), 1)
    up, down, right = col // (inner * inner), (col // inner) % inner, col % inner
    flat = tensor_ref[...].astype(F32)
    value = jnp.zeros((inner, wide), F32)
    total = jnp.zeros((inner, wide), jnp.int32)
    for v in range(inner):
        value = jnp.where(row == v, flat[:, v * wide : (v + 1) * wide], value)
        total = total + jnp.where(row == v, charges_ref[0, v], 0)
        total = total + jnp.where(up == v, charges_ref[1, v], 0)
        total = total - jnp.where(down == v, charges_ref[2, v], 0)
        total = total - jnp.where(right == v, charges_ref[3, v], 0)
    total = total + 6
    value = jnp.where(total % 3 == 0, value, 0.0)
    block = inner * group
    full = inner * block
    tiled = jnp.concatenate([value] * (full // inner), axis=0)
    down_of_row = iota((full, wide), 0) // block
    down_of_col = (iota((full, wide), 1) // inner) % inner
    tiled = jnp.where(down_of_row == down_of_col, tiled, 0.0).astype(BF16)
    src, dst = iota((wide, full), 0), iota((wide, full), 1)
    same_up = src // (inner * inner) == dst % inner
    same_right = src % inner == dst // block
    pick = jnp.where(same_up & same_right, 1.0, 0.0).astype(BF16)
    spread = dot(tiled, pick)
    a_row = (iota((full, full), 0) // inner) % group
    a_col = (iota((full, full), 1) // inner) % group
    return jnp.where(a_row == a_col, spread, 0.0)


def kernel(
    outer,
    inner,
    envs,
    start_ref,
    kept_ref,
    charges_ref,
    tensor_ref,
    initial_hbm,
    right_hbm,
    left_hbm,
    out_ref,
    initial_v,
    chosen,
    raw,
    right_v,
    left_own,
    left_in,
    half,
    sites,
    acc,
    operator,
    outgoing,
    arrived,
    load_sem,
    initial_sem,
    left_send,
    left_recv,
    send_sem,
    recv_sem,
):
    rows, cols = lax.axis_size("row"), lax.axis_size("col")
    row, col = lax.axis_index("row"), lax.axis_index("col")
    right_col = lax.rem(col + 1, cols)
    left_col = lax.rem(col + cols - 1, cols)
    size = outer * inner
    part = size // CHUNKS
    keys = outer // CHUNKS
    full = outer
    lanes = full // 2
    group = full // (inner * inner)
    block = group * inner
    pairs = inner // 2
    has_next = row < rows - 1
    has_before = row > 0

    load_left = pltpu.make_async_copy(left_hbm, raw.at[0], load_sem.at[0])
    load_right = pltpu.make_async_copy(right_hbm, raw.at[1], load_sem.at[1])
    load_left.start()
    load_right.start()

    def load_initial(i):
        span = pl.ds(i * part, part)
        return pltpu.make_async_copy(initial_hbm.at[:, span, :], initial_v.at[:, span, :], initial_sem.at[i])

    for i in range(CHUNKS):
        load_initial(i).start()

    barrier = pltpu.get_barrier_semaphore()
    pl.semaphore_signal(barrier, inc=1, device_id=(row, right_col), device_id_type=MESH)
    pl.semaphore_signal(barrier, inc=1, device_id=(row, left_col), device_id_type=MESH)

    @pl.when(has_next)
    def _():
        pl.semaphore_signal(barrier, inc=1, device_id=(row + 1, col), device_id_type=MESH)

    @pl.when(has_before)
    def _():
        pl.semaphore_signal(barrier, inc=1, device_id=(row - 1, col), device_id_type=MESH)

    kept = kept_ref[0, 0]
    operator[...] = block_operator(tensor_ref, charges_ref, inner, group).astype(BF16)

    load_left.wait()
    to, frm = iota((full, full), 0), iota((full, full), 1)
    keep_eye = jnp.where((to == frm) & (to < kept), 1.0, 0.0).astype(BF16)
    for i in range(CHUNKS):
        left_own[:, i * part : (i + 1) * part] = dot_t(keep_eye, raw[0, i * part : (i + 1) * part, :]).astype(BF16)

    pl.semaphore_wait(barrier, 2 + jnp.where(has_next, 1, 0) + jnp.where(has_before, 1, 0))

    def left_copy(i):
        span = pl.ds(i * (outer // LEFT_PARTS), outer // LEFT_PARTS)
        return pltpu.make_async_remote_copy(
            src_ref=left_own.at[span, :],
            dst_ref=left_in.at[span, :],
            send_sem=left_send.at[i],
            recv_sem=left_recv.at[i],
            device_id=(row, right_col),
            device_id_type=MESH,
        )

    for i in range(LEFT_PARTS):
        left_copy(i).start()

    def boundary_copy(step, h, i):
        span = pl.ds(i * part, part)
        return pltpu.make_async_remote_copy(
            src_ref=outgoing.at[step, h, span, :],
            dst_ref=arrived.at[step, h, span, :],
            send_sem=send_sem.at[step, h, i],
            recv_sem=recv_sem.at[step, h, i],
            device_id=(row + 1, col),
            device_id_type=MESH,
        )

    load_right.wait()
    split = jnp.where(frm == (to % keys) * inner + to // keys, 1.0, 0.0).astype(BF16)
    merge = jnp.where(frm == (to % inner) * keys + to // inner, 1.0, 0.0).astype(BF16)
    inside = frm < kept
    for i in range(CHUNKS):
        moved = dot(split, raw[1, i * part : (i + 1) * part, :])
        moved = jnp.where(inside, moved, 0.0).astype(BF16)
        for s in range(inner):
            for h in range(2):
                right_v[h, s // 2, i * keys : (i + 1) * keys, (s % 2) * lanes : (s % 2 + 1) * lanes] = moved[
                    s * keys : (s + 1) * keys, h * lanes : (h + 1) * lanes
                ]

    def absorb_sites(x, h, i):
        for p in range(pairs):
            y = dot(x, right_v[h, p]).astype(BF16)
            half[h, 2 * p] = y[:, :lanes]
            half[h, 2 * p + 1] = y[:, lanes:]
        for g in range(0, keys // group, 2):
            sides = [half[h, :, (g + n) * block : (g + n + 1) * block, :].reshape(full, lanes) for n in range(2)]
            y = dot(operator[...], jnp.concatenate(sides, axis=1)).astype(BF16)
            for d in range(inner):
                for n in range(2):
                    sites[h, d // 2, pl.ds(i * part + (g + n) * block, block), (d % 2) * lanes : (d % 2 + 1) * lanes] = y[
                        d * block : (d + 1) * block, n * lanes : (n + 1) * lanes
                    ]

    def merged(h, i):
        span = pl.ds(i * keys, keys)
        stacked = [acc[h, d // 2, span, (d % 2) * lanes : (d % 2 + 1) * lanes] for d in range(inner)]
        return dot(merge, jnp.concatenate(stacked, axis=0).astype(BF16)).astype(BF16)

    flags = [jnp.where(start_ref[e] == row, 1.0, 0.0) for e in range(envs)]

    def choose(i, carry):
        load_initial(i).wait()
        span = pl.ds(pl.multiple_of(i * part, part), part)
        x = initial_v[0, span, :] * jnp.full((part, outer), flags[0], F32).astype(BF16)
        for e in range(1, envs):
            x = x + initial_v[e, span, :] * jnp.full((part, outer), flags[e], F32).astype(BF16)
        chosen[span, :] = x
        absorb_sites(x, 0, i)
        return carry

    lax.fori_loop(0, CHUNKS, choose, 0)

    def give_first(h):
        for p in range(pairs):
            acc[h, p] = dot(left_in[...], sites[h, p])
        for i in range(CHUNKS):
            outgoing[0, h, i * part : (i + 1) * part, :] = merged(h, i)

            @pl.when(has_next)
            def _(i=i):
                boundary_copy(0, h, i).start()

    for i in range(LEFT_PARTS):
        left_copy(i).wait_recv()
    give_first(0)

    def second(i, carry):
        span = pl.ds(pl.multiple_of(i * part, part), part)
        absorb_sites(chosen[span, :], 1, i)
        return carry

    lax.fori_loop(0, CHUNKS, second, 0)
    give_first(1)

    @pl.when(jnp.logical_not(has_before))
    def _():
        arrived[...] = jnp.zeros_like(arrived)

    for step in range(1, ABSORB):

        def take(i, carry, step=step):
            @pl.when(has_before)
            def _():
                for h in range(2):
                    boundary_copy(step - 1, h, i).wait_recv()

            span = pl.ds(pl.multiple_of(i * part, part), part)
            x = jnp.concatenate([arrived[step - 1, h, span, :] for h in range(2)], axis=1)
            for h in range(2):
                absorb_sites(x, h, i)
            for h in range(2):
                for p in range(pairs):
                    acc[h, p] += dot(left_in[:, span], sites[h, p, span, :])
            return carry

        acc[...] = jnp.zeros_like(acc)
        lax.fori_loop(0, CHUNKS, take, 0)

        for i in range(CHUNKS):
            for h in range(2):
                if step < ABSORB - 1:
                    outgoing[step, h, i * part : (i + 1) * part, :] = merged(h, i)

                    @pl.when(has_next)
                    def _(i=i, h=h, step=step):
                        boundary_copy(step, h, i).start()

                else:
                    out_ref[i * part : (i + 1) * part, h * lanes : (h + 1) * lanes] = merged(h, i)

    for i in range(LEFT_PARTS):
        left_copy(i).wait_send()

    @pl.when(has_next)
    def _():
        for step in range(ABSORB - 1):
            for h in range(2):
                for i in range(CHUNKS):
                    boundary_copy(step, h, i).wait_send()


def shards(start_rows, initial, site_tensors, charges, right_proj, left_proj, kept_ranks):
    envs, _, outer, inner, _ = initial.shape
    size = outer * inner
    smem = pl.BlockSpec(memory_space=pltpu.SMEM)
    vmem = pl.BlockSpec(memory_space=pltpu.VMEM)
    hbm = pl.BlockSpec(memory_space=pl.ANY)
    out = pl.pallas_call(
        functools.partial(kernel, outer, inner, envs),
        out_shape=jax.ShapeDtypeStruct((size, outer), BF16),
        in_specs=[smem, smem, smem, vmem, hbm, hbm, hbm],
        out_specs=vmem,
        scratch_shapes=[
            pltpu.VMEM((envs, size, outer), BF16),
            pltpu.VMEM((size, outer), BF16),
            pltpu.VMEM((2, size, outer), BF16),
            pltpu.VMEM((2, inner // 2, outer, outer), BF16),
            pltpu.VMEM((outer, size), BF16),
            pltpu.VMEM((outer, size), BF16),
            pltpu.VMEM((2, inner, size // CHUNKS, outer // 2), BF16),
            pltpu.VMEM((2, inner // 2, size, outer), BF16),
            pltpu.VMEM((2, inner // 2, outer, outer), F32),
            pltpu.VMEM((outer, outer), BF16),
            pltpu.VMEM((ABSORB - 1, 2, size, outer // 2), BF16),
            pltpu.VMEM((ABSORB - 1, 2, size, outer // 2), BF16),
            pltpu.SemaphoreType.DMA((2,)),
            pltpu.SemaphoreType.DMA((CHUNKS,)),
            pltpu.SemaphoreType.DMA((LEFT_PARTS,)),
            pltpu.SemaphoreType.DMA((LEFT_PARTS,)),
            pltpu.SemaphoreType.DMA((ABSORB - 1, 2, CHUNKS)),
            pltpu.SemaphoreType.DMA((ABSORB - 1, 2, CHUNKS)),
        ],
        compiler_params=pltpu.CompilerParams(
            collective_id=0, has_side_effects=True, vmem_limit_bytes=56 * 1024 * 1024
        ),
        cost_estimate=pl.CostEstimate(
            flops=ABSORB * 6 * size * size * outer, bytes_accessed=8 * size * outer * 2, transcendentals=0
        ),
    )(
        start_rows,
        kept_ranks,
        charges[0, 0],
        site_tensors[0],
        initial.reshape(envs, size, outer),
        right_proj.reshape(size, outer),
        left_proj.reshape(size, outer),
    )
    return out.reshape(1, 1, outer, inner, outer)


def solution(mesh):
    return jax.shard_map(
        shards,
        mesh=mesh,
        in_specs=(
            P(),
            P(None, "col", None, None, None),
            P("row", "col", None),
            P("row", "col", None, None),
            P("row", "col", None, None, None),
            P("row", "col", None, None, None),
            P("row", "col"),
        ),
        out_specs=P("row", "col", None, None, None),
        check_vma=False,
    )
```

time: 73.7 us -> 71.2 us (0.966)
  Pallas kernels: 69.4 us -> 67.4 us
    pallas_call x1, Pallas kernels: 69.4 us -> 67.4 us  [shards(): pl.pallas_call(functools.partial(kernel, outer, inner, envs), out_shape=j...]
where the time goes in v1:
time: 71.2 us; the launch traced here: 70.3 us
  Pallas kernels  67.4 us (95%)
  local copies, waits for them, and re-layouts  2.26 us (3%)
    pallas_call x1, Pallas kernels, shards(): pl.pallas_call(functools.partial(kernel, outer, inner, envs), out_shape=j...  67.4 us
    unnamed x1, local copies, waits for them, and re-layouts  2.26 us

profile of v1, /device:TPU:16, one launch (start us, length us, event | category | flops | bytes accessed | tf_op | source)
XLA Modules:
  0.0 70.3 jit_solution(17724883604788728624)
XLA Ops:
  0.7 67.4 %shard_map.73 = bf16[2048,256]{1,0:T(8,128)(2,1)} custom-call(s32[4]{0:T(128)} %start_ref.1, s32[1,1]{1,0:T(1,128)S(6)} %copy.9.kept_ref, s32[4,8]{1,0:T(4,128)} %bitcast.11, bf16[1,4096]{1,0:T(2,128)(2,1)} %bitcast.10, bf16[4,2048,256]{2,1,0:T(8,128)(2,1)} %bitcast.7, bf16[2048,256]{1,0:T(8,128)(2,1)} %bitcast.8, bf16[2048,256]{1,0:T(8,128)(2,1)} %bitcast.9), custom_call_target="tpu_custom_call" | custom-call | flops 19327352832 | bytes 8388608 | tf_op jit(solution)/shard_map/pallas_call | solution.py:289
  68.1 2.3 %copy.10 = bf16[1,1,256,8,256]{4,3,2,1,0:T(8,128)(2,1)} copy(bf16[1,1,256,8,256]{4,3,2,1,0:T(8,128)(2,1)} %bitcast.6) | data formatting | bytes 2097152

commit v2 on v1

--- a/solution.py
+++ b/solution.py
@@ -66,11 +66,12 @@
     start_ref,
     kept_ref,
     charges_ref,
-    tensor_ref,
+    tensor_hbm,
     initial_hbm,
     right_hbm,
     left_hbm,
     out_ref,
+    tensor_ref,
     initial_v,
     chosen,
     raw,
@@ -109,36 +110,33 @@
     load_right = pltpu.make_async_copy(right_hbm, raw.at[1], load_sem.at[1])
     load_left.start()
     load_right.start()
+    load_tensor = pltpu.make_async_copy(tensor_hbm, tensor_ref, load_sem.at[2])
+    load_tensor.start()
 
     def load_initial(i):
-        span = pl.ds(i * part, part)
+        span = pl.ds(i * 2 * part, 2 * part)
         return pltpu.make_async_copy(initial_hbm.at[:, span, :], initial_v.at[:, span, :], initial_sem.at[i])
 
-    for i in range(CHUNKS):
-        load_initial(i).start()
-
     barrier = pltpu.get_barrier_semaphore()
-    pl.semaphore_signal(barrier, inc=1, device_id=(row, right_col), device_id_type=MESH)
     pl.semaphore_signal(barrier, inc=1, device_id=(row, left_col), device_id_type=MESH)
-
-    @pl.when(has_next)
-    def _():
-        pl.semaphore_signal(barrier, inc=1, device_id=(row + 1, col), device_id_type=MESH)
 
     @pl.when(has_before)
     def _():
         pl.semaphore_signal(barrier, inc=1, device_id=(row - 1, col), device_id_type=MESH)
 
     kept = kept_ref[0, 0]
+    load_tensor.wait()
     operator[...] = block_operator(tensor_ref, charges_ref, inner, group).astype(BF16)
 
     load_left.wait()
+    for i in range(CHUNKS // 2):
+        load_initial(i).start()
     to, frm = iota((full, full), 0), iota((full, full), 1)
     keep_eye = jnp.where((to == frm) & (to < kept), 1.0, 0.0).astype(BF16)
     for i in range(CHUNKS):
         left_own[:, i * part : (i + 1) * part] = dot_t(keep_eye, raw[0, i * part : (i + 1) * part, :]).astype(BF16)
 
-    pl.semaphore_wait(barrier, 2 + jnp.where(has_next, 1, 0) + jnp.where(has_before, 1, 0))
+    pl.semaphore_wait(barrier, 1 + jnp.where(has_next, 1, 0))
 
     def left_copy(i):
         span = pl.ds(i * (outer // LEFT_PARTS), outer // LEFT_PARTS)
@@ -178,17 +176,18 @@
                     s * keys : (s + 1) * keys, h * lanes : (h + 1) * lanes
                 ]
 
-    def absorb_sites(x, h, i):
+    def absorb_sites(x, h, at):
+        count = x.shape[0]
         for p in range(pairs):
             y = dot(x, right_v[h, p]).astype(BF16)
-            half[h, 2 * p] = y[:, :lanes]
-            half[h, 2 * p + 1] = y[:, lanes:]
-        for g in range(0, keys // group, 2):
+            half[h, 2 * p, :count] = y[:, :lanes]
+            half[h, 2 * p + 1, :count] = y[:, lanes:]
+        for g in range(0, count // block, 2):
             sides = [half[h, :, (g + n) * block : (g + n + 1) * block, :].reshape(full, lanes) for n in range(2)]
             y = dot(operator[...], jnp.concatenate(sides, axis=1)).astype(BF16)
             for d in range(inner):
                 for n in range(2):
-                    sites[h, d // 2, pl.ds(i * part + (g + n) * block, block), (d % 2) * lanes : (d % 2 + 1) * lanes] = y[
+                    sites[h, d // 2, pl.ds(at + (g + n) * block, block), (d % 2) * lanes : (d % 2 + 1) * lanes] = y[
                         d * block : (d + 1) * block, n * lanes : (n + 1) * lanes
                     ]
 
@@ -201,15 +200,16 @@
 
     def choose(i, carry):
         load_initial(i).wait()
-        span = pl.ds(pl.multiple_of(i * part, part), part)
-        x = initial_v[0, span, :] * jnp.full((part, outer), flags[0], F32).astype(BF16)
+        at = pl.multiple_of(i * 2 * part, 2 * part)
+        span = pl.ds(at, 2 * part)
+        x = initial_v[0, span, :] * jnp.full((2 * part, outer), flags[0], F32).astype(BF16)
         for e in range(1, envs):
-            x = x + initial_v[e, span, :] * jnp.full((part, outer), flags[e], F32).astype(BF16)
+            x = x + initial_v[e, span, :] * jnp.full((2 * part, outer), flags[e], F32).astype(BF16)
         chosen[span, :] = x
-        absorb_sites(x, 0, i)
+        absorb_sites(x, 0, at)
         return carry
 
-    lax.fori_loop(0, CHUNKS, choose, 0)
+    lax.fori_loop(0, CHUNKS // 2, choose, 0)
 
     def give_first(h):
         for p in range(pairs):
@@ -226,11 +226,11 @@
     give_first(0)
 
     def second(i, carry):
-        span = pl.ds(pl.multiple_of(i * part, part), part)
-        absorb_sites(chosen[span, :], 1, i)
+        at = pl.multiple_of(i * 2 * part, 2 * part)
+        absorb_sites(chosen[pl.ds(at, 2 * part), :], 1, at)
         return carry
 
-    lax.fori_loop(0, CHUNKS, second, 0)
+    lax.fori_loop(0, CHUNKS // 2, second, 0)
     give_first(1)
 
     @pl.when(jnp.logical_not(has_before))
@@ -239,35 +239,38 @@
 
     for step in range(1, ABSORB):
 
-        def take(i, carry, step=step):
+        def take(i, carry, step=step, count=2):
             @pl.when(has_before)
             def _():
-                for h in range(2):
-                    boundary_copy(step - 1, h, i).wait_recv()
-
-            span = pl.ds(pl.multiple_of(i * part, part), part)
+                for n in range(count):
+                    for h in range(2):
+                        boundary_copy(step - 1, h, i * count + n).wait_recv()
+
+            at = pl.multiple_of(i * count * part, count * part)
+            span = pl.ds(at, count * part)
             x = jnp.concatenate([arrived[step - 1, h, span, :] for h in range(2)], axis=1)
             for h in range(2):
-                absorb_sites(x, h, i)
+                absorb_sites(x, h, at)
             for h in range(2):
                 for p in range(pairs):
                     acc[h, p] += dot(left_in[:, span], sites[h, p, span, :])
             return carry
 
         acc[...] = jnp.zeros_like(acc)
-        lax.fori_loop(0, CHUNKS, take, 0)
+        lax.fori_loop(0, CHUNKS // 2 - 1, take, 0)
+        lax.fori_loop(CHUNKS - 2, CHUNKS, functools.partial(take, count=1), 0)
 
         for i in range(CHUNKS):
-            for h in range(2):
-                if step < ABSORB - 1:
+            if step < ABSORB - 1:
+                for h in range(2):
                     outgoing[step, h, i * part : (i + 1) * part, :] = merged(h, i)
 
                     @pl.when(has_next)
                     def _(i=i, h=h, step=step):
                         boundary_copy(step, h, i).start()
 
-                else:
-                    out_ref[i * part : (i + 1) * part, h * lanes : (h + 1) * lanes] = merged(h, i)
+            else:
+                out_ref[i * part : (i + 1) * part, :] = jnp.concatenate([merged(h, i) for h in range(2)], axis=1)
 
     for i in range(LEFT_PARTS):
         left_copy(i).wait_send()
@@ -285,34 +288,35 @@
     size = outer * inner
     smem = pl.BlockSpec(memory_space=pltpu.SMEM)
     vmem = pl.BlockSpec(memory_space=pltpu.VMEM)
-    hbm = pl.BlockSpec(memory_space=pl.ANY)
+    hbm = pl.BlockSpec(memory_space=pltpu.HBM)
     out = pl.pallas_call(
         functools.partial(kernel, outer, inner, envs),
-        out_shape=jax.ShapeDtypeStruct((size, outer), BF16),
-        in_specs=[smem, smem, smem, vmem, hbm, hbm, hbm],
+        out_shape=pltpu.VMEM((size, outer), BF16),
+        in_specs=[smem, smem, smem, hbm, hbm, hbm, hbm],
         out_specs=vmem,
         scratch_shapes=[
+            pltpu.VMEM((1, inner**4), BF16),
             pltpu.VMEM((envs, size, outer), BF16),
             pltpu.VMEM((size, outer), BF16),
             pltpu.VMEM((2, size, outer), BF16),
             pltpu.VMEM((2, inner // 2, outer, outer), BF16),
             pltpu.VMEM((outer, size), BF16),
             pltpu.VMEM((outer, size), BF16),
-            pltpu.VMEM((2, inner, size // CHUNKS, outer // 2), BF16),
+            pltpu.VMEM((2, inner, 2 * size // CHUNKS, outer // 2), BF16),
             pltpu.VMEM((2, inner // 2, size, outer), BF16),
             pltpu.VMEM((2, inner // 2, outer, outer), F32),
             pltpu.VMEM((outer, outer), BF16),
             pltpu.VMEM((ABSORB - 1, 2, size, outer // 2), BF16),
             pltpu.VMEM((ABSORB - 1, 2, size, outer // 2), BF16),
-            pltpu.SemaphoreType.DMA((2,)),
-            pltpu.SemaphoreType.DMA((CHUNKS,)),
+            pltpu.SemaphoreType.DMA((3,)),
+            pltpu.SemaphoreType.DMA((CHUNKS // 2,)),
             pltpu.SemaphoreType.DMA((LEFT_PARTS,)),
             pltpu.SemaphoreType.DMA((LEFT_PARTS,)),
             pltpu.SemaphoreType.DMA((ABSORB - 1, 2, CHUNKS)),
             pltpu.SemaphoreType.DMA((ABSORB - 1, 2, CHUNKS)),
         ],
         compiler_params=pltpu.CompilerParams(
-            collective_id=0, has_side_effects=True, vmem_limit_bytes=56 * 1024 * 1024
+            collective_id=0, has_side_effects=True, vmem_limit_bytes=58 * 1024 * 1024
         ),
         cost_estimate=pl.CostEstimate(
             flops=ABSORB * 6 * size * size * outer, bytes_accessed=8 * size * outer * 2, transcendentals=0

time: 71.2 us -> 69.1 us (0.971)
  local copies, waits for them, and re-layouts: 2.26 us -> 0.97 us
  Pallas kernels: 67.4 us -> 66.3 us
    unnamed x1, local copies, waits for them, and re-layouts: 2.26 us -> 0.97 us
    pallas_call x1, Pallas kernels: 67.4 us -> 66.3 us  [shards(): pl.pallas_call(functools.partial(kernel, outer, inner, envs), out_shape=p...]
where the time goes in v2:
time: 69.1 us; the launch traced here: 67.9 us
  Pallas kernels  66.3 us (96%)
  local copies, waits for them, and re-layouts  0.97 us (1%)
    pallas_call x1, Pallas kernels, shards(): pl.pallas_call(functools.partial(kernel, outer, inner, envs), out_shape=p...  66.3 us

profile of v2, /device:TPU:16, one launch (start us, length us, event | category | flops | bytes accessed | tf_op | source)
XLA Modules:
  0.0 67.9 jit_solution(7120805655699458822)
XLA Ops:
  0.7 66.3 %shard_map.73 = bf16[2048,256]{1,0:T(8,128)(2,1)S(1)} custom-call(s32[4]{0:T(128)} %start_ref.1, s32[1,1]{1,0:T(1,128)S(6)} %copy.10.kept_ref, s32[4,8]{1,0:T(4,128)} %bitcast.11, bf16[1,4096]{1,0:T(2,128)(2,1)} %bitcast.10, bf16[4,2048,256]{2,1,0:T(8,128)(2,1)} %bitcast.7, bf16[2048,256]{1,0:T(8,128)(2,1)} %bitcast.8, bf16[2048,256]{1,0:T(8,128)(2,1)} %bitcast.9), custom_call_target="tpu_custom_call" | custom-call | flops 19327352832 | bytes 8388608 | tf_op jit(solution)/shard_map/pallas_call | solution.py:292
  67.0 1.0 %copy.9 = bf16[1,1,256,8,256]{4,3,2,1,0:T(8,128)(2,1)} copy(bf16[1,1,256,8,256]{4,3,2,1,0:T(8,128)(2,1)S(1)} %bitcast.6) | data formatting | bytes 2097152

commit v3 on v2

--- a/solution.py
+++ b/solution.py
@@ -90,6 +90,9 @@
     left_recv,
     send_sem,
     recv_sem,
+    passing,
+    relay_send,
+    relay_recv,
 ):
     rows, cols = lax.axis_size("row"), lax.axis_size("col")
     row, col = lax.axis_index("row"), lax.axis_index("col")
@@ -103,8 +106,18 @@
     group = full // (inner * inner)
     block = group * inner
     pairs = inner // 2
-    has_next = row < rows - 1
-    has_before = row > 0
+
+    def working(step):
+        return (row >= step) & (row <= rows - ABSORB + step)
+
+    cross = rows // 2 - 1
+    crosses = row == cross
+    relays = row == rows - 1
+    lands = row == cross + 1
+    far_col = lax.rem(col + cols // 2, cols)
+    sends_any = row < rows - 1
+    receives_any = row > 0
+    odd = lax.rem(col, 2) == 1
 
     load_left = pltpu.make_async_copy(left_hbm, raw.at[0], load_sem.at[0])
     load_right = pltpu.make_async_copy(right_hbm, raw.at[1], load_sem.at[1])
@@ -117,26 +130,30 @@
         span = pl.ds(i * 2 * part, 2 * part)
         return pltpu.make_async_copy(initial_hbm.at[:, span, :], initial_v.at[:, span, :], initial_sem.at[i])
 
+    load_initial(0).start()
+
     barrier = pltpu.get_barrier_semaphore()
     pl.semaphore_signal(barrier, inc=1, device_id=(row, left_col), device_id_type=MESH)
 
-    @pl.when(has_before)
+    @pl.when(receives_any)
     def _():
         pl.semaphore_signal(barrier, inc=1, device_id=(row - 1, col), device_id_type=MESH)
 
+    @pl.when(relays)
+    def _():
+        pl.semaphore_signal(barrier, inc=1, device_id=(cross, far_col), device_id_type=MESH)
+
+    @pl.when(lands)
+    def _():
+        pl.semaphore_signal(barrier, inc=1, device_id=(rows - 1, far_col), device_id_type=MESH)
+
     kept = kept_ref[0, 0]
-    load_tensor.wait()
-    operator[...] = block_operator(tensor_ref, charges_ref, inner, group).astype(BF16)
-
     load_left.wait()
-    for i in range(CHUNKS // 2):
-        load_initial(i).start()
+    load_initial(1).start()
     to, frm = iota((full, full), 0), iota((full, full), 1)
     keep_eye = jnp.where((to == frm) & (to < kept), 1.0, 0.0).astype(BF16)
     for i in range(CHUNKS):
         left_own[:, i * part : (i + 1) * part] = dot_t(keep_eye, raw[0, i * part : (i + 1) * part, :]).astype(BF16)
-
-    pl.semaphore_wait(barrier, 1 + jnp.where(has_next, 1, 0))
 
     def left_copy(i):
         span = pl.ds(i * (outer // LEFT_PARTS), outer // LEFT_PARTS)
@@ -149,6 +166,7 @@
             device_id_type=MESH,
         )
 
+    pl.semaphore_wait(barrier, 1 + jnp.where(sends_any, 1, 0) + jnp.where(crosses, 1, 0) + jnp.where(relays, 1, 0))
     for i in range(LEFT_PARTS):
         left_copy(i).start()
 
@@ -162,6 +180,48 @@
             device_id=(row + 1, col),
             device_id_type=MESH,
         )
+
+    def to_relay(step, i):
+        span = pl.ds(i * part, part)
+        return pltpu.make_async_remote_copy(
+            src_ref=outgoing.at[step, 1, span, :],
+            dst_ref=passing.at[step, span, :],
+            send_sem=send_sem.at[step, 1, i],
+            recv_sem=relay_recv.at[step, i],
+            device_id=(rows - 1, far_col),
+            device_id_type=MESH,
+        )
+
+    def from_relay(step, i):
+        span = pl.ds(i * part, part)
+        return pltpu.make_async_remote_copy(
+            src_ref=passing.at[step, span, :],
+            dst_ref=arrived.at[step, 1, span, :],
+            send_sem=relay_send.at[step, i],
+            recv_sem=recv_sem.at[step, 1, i],
+            device_id=(cross + 1, far_col),
+            device_id_type=MESH,
+        )
+
+    def pass_on(step, i):
+        to_relay(step, i).wait_recv()
+        from_relay(step, i).start()
+
+    def give(step, h, i):
+        if h == 0:
+            boundary_copy(step, 0, i).start()
+        else:
+
+            @pl.when(crosses)
+            def _():
+                to_relay(step, i).start()
+
+            @pl.when(jnp.logical_not(crosses))
+            def _():
+                boundary_copy(step, 1, i).start()
+
+    load_tensor.wait()
+    operator[...] = block_operator(tensor_ref, charges_ref, inner, group).astype(BF16)
 
     load_right.wait()
     split = jnp.where(frm == (to % keys) * inner + to // keys, 1.0, 0.0).astype(BF16)
@@ -191,15 +251,23 @@
                         d * block : (d + 1) * block, n * lanes : (n + 1) * lanes
                     ]
 
-    def merged(h, i):
+    def merged(halves, i):
         span = pl.ds(i * keys, keys)
-        stacked = [acc[h, d // 2, span, (d % 2) * lanes : (d % 2 + 1) * lanes] for d in range(inner)]
-        return dot(merge, jnp.concatenate(stacked, axis=0).astype(BF16)).astype(BF16)
+        sides = []
+        for h in halves:
+            stacked = [acc[h, d // 2, span, (d % 2) * lanes : (d % 2 + 1) * lanes] for d in range(inner)]
+            sides.append(jnp.concatenate(stacked, axis=0).astype(BF16))
+        return dot(merge, jnp.concatenate(sides, axis=1)).astype(BF16)
 
     flags = [jnp.where(start_ref[e] == row, 1.0, 0.0) for e in range(envs)]
 
     def choose(i, carry):
         load_initial(i).wait()
+
+        @pl.when(i < CHUNKS // 2 - 2)
+        def _():
+            load_initial(i + 2).start()
+
         at = pl.multiple_of(i * 2 * part, 2 * part)
         span = pl.ds(at, 2 * part)
         x = initial_v[0, span, :] * jnp.full((2 * part, outer), flags[0], F32).astype(BF16)
@@ -215,36 +283,41 @@
         for p in range(pairs):
             acc[h, p] = dot(left_in[...], sites[h, p])
         for i in range(CHUNKS):
-            outgoing[0, h, i * part : (i + 1) * part, :] = merged(h, i)
-
-            @pl.when(has_next)
+            outgoing[0, h, i * part : (i + 1) * part, :] = merged((h,), i)
+
+            @pl.when(working(0))
             def _(i=i):
-                boundary_copy(0, h, i).start()
-
-    for i in range(LEFT_PARTS):
-        left_copy(i).wait_recv()
-    give_first(0)
+                give(0, h, i)
+
+    @pl.when(relays)
+    def _():
+        for i in range(CHUNKS):
+            pass_on(0, i)
 
     def second(i, carry):
         at = pl.multiple_of(i * 2 * part, 2 * part)
         absorb_sites(chosen[pl.ds(at, 2 * part), :], 1, at)
         return carry
 
-    lax.fori_loop(0, CHUNKS // 2, second, 0)
+    @pl.when(jnp.logical_not(odd))
+    def _():
+        lax.fori_loop(0, CHUNKS // 2, second, 0)
+
+    for i in range(LEFT_PARTS):
+        left_copy(i).wait_recv()
+    give_first(0)
+
+    @pl.when(odd)
+    def _():
+        lax.fori_loop(0, CHUNKS // 2, second, 0)
+
     give_first(1)
 
-    @pl.when(jnp.logical_not(has_before))
-    def _():
-        arrived[...] = jnp.zeros_like(arrived)
-
-    for step in range(1, ABSORB):
-
-        def take(i, carry, step=step, count=2):
-            @pl.when(has_before)
-            def _():
-                for n in range(count):
-                    for h in range(2):
-                        boundary_copy(step - 1, h, i * count + n).wait_recv()
+    def later(step):
+        def take(i, carry, count=2):
+            for n in range(count):
+                for h in range(2):
+                    boundary_copy(step - 1, h, i * count + n).wait_recv()
 
             at = pl.multiple_of(i * count * part, count * part)
             span = pl.ds(at, count * part)
@@ -256,31 +329,51 @@
                     acc[h, p] += dot(left_in[:, span], sites[h, p, span, :])
             return carry
 
+        if step == ABSORB - 1:
+
+            @pl.when(relays)
+            def _():
+                for i in range(CHUNKS):
+                    pass_on(step - 1, i)
+
         acc[...] = jnp.zeros_like(acc)
         lax.fori_loop(0, CHUNKS // 2 - 1, take, 0)
         lax.fori_loop(CHUNKS - 2, CHUNKS, functools.partial(take, count=1), 0)
 
         for i in range(CHUNKS):
+            made = merged((0, 1), i)
             if step < ABSORB - 1:
                 for h in range(2):
-                    outgoing[step, h, i * part : (i + 1) * part, :] = merged(h, i)
-
-                    @pl.when(has_next)
-                    def _(i=i, h=h, step=step):
-                        boundary_copy(step, h, i).start()
-
+                    outgoing[step, h, i * part : (i + 1) * part, :] = made[:, h * lanes : (h + 1) * lanes]
+                    give(step, h, i)
             else:
-                out_ref[i * part : (i + 1) * part, :] = jnp.concatenate([merged(h, i) for h in range(2)], axis=1)
+                out_ref[i * part : (i + 1) * part, :] = made
+
+    for step in range(1, ABSORB):
+
+        @pl.when(working(step))
+        def _(step=step):
+            later(step)
+
+    @pl.when(jnp.logical_not(working(ABSORB - 1)))
+    def _():
+        out_ref[...] = jnp.zeros_like(out_ref)
 
     for i in range(LEFT_PARTS):
         left_copy(i).wait_send()
 
-    @pl.when(has_next)
-    def _():
-        for step in range(ABSORB - 1):
+    for step in range(ABSORB - 1):
+
+        @pl.when(working(step))
+        def _(step=step):
             for h in range(2):
                 for i in range(CHUNKS):
                     boundary_copy(step, h, i).wait_send()
+
+        @pl.when(relays)
+        def _(step=step):
+            for i in range(CHUNKS):
+                from_relay(step, i).wait_send()
 
 
 def shards(start_rows, initial, site_tensors, charges, right_proj, left_proj, kept_ranks):
@@ -314,6 +407,9 @@
             pltpu.SemaphoreType.DMA((LEFT_PARTS,)),
             pltpu.SemaphoreType.DMA((ABSORB - 1, 2, CHUNKS)),
             pltpu.SemaphoreType.DMA((ABSORB - 1, 2, CHUNKS)),
+            pltpu.VMEM((ABSORB - 1, size, outer // 2), BF16),
+            pltpu.SemaphoreType.DMA((ABSORB - 1, CHUNKS)),
+            pltpu.SemaphoreType.DMA((ABSORB - 1, CHUNKS)),
         ],
         compiler_params=pltpu.CompilerParams(
             collective_id=0, has_side_effects=True, vmem_limit_bytes=58 * 1024 * 1024

time: 69.1 us -> 65.4 us (0.946); the launches traced: 67.9 us -> 65.3 us
  Pallas kernels: 66.3 us -> 63.6 us
    pallas_call x1, Pallas kernels: 66.3 us -> 63.6 us  [shards(): pl.pallas_call(functools.partial(kernel, outer, inner, envs), out_shape=p...]
where the time goes in v3:
time: 65.4 us; the launch traced here: 65.3 us
  Pallas kernels  63.6 us (97%)
  local copies, waits for them, and re-layouts  0.97 us (1%)
  between operations  0.66 us (1%)
    pallas_call x1, Pallas kernels, shards(): pl.pallas_call(functools.partial(kernel, outer, inner, envs), out_shape=p...  63.6 us

profile of v3, /device:TPU:16, one launch (start us, length us, event | category | flops | bytes accessed | tf_op | source)
XLA Modules:
  0.0 65.3 jit_solution(15473644867992801762)
XLA Ops:
  0.7 63.6 %shard_map.73 = bf16[2048,256]{1,0:T(8,128)(2,1)S(1)} custom-call(s32[4]{0:T(128)} %start_ref.1, s32[1,1]{1,0:T(1,128)S(6)} %copy.10.kept_ref, s32[4,8]{1,0:T(4,128)} %bitcast.11, bf16[1,4096]{1,0:T(2,128)(2,1)} %bitcast.10, bf16[4,2048,256]{2,1,0:T(8,128)(2,1)} %bitcast.7, bf16[2048,256]{1,0:T(8,128)(2,1)} %bitcast.8, bf16[2048,256]{1,0:T(8,128)(2,1)} %bitcast.9), custom_call_target="tpu_custom_call" | custom-call | flops 19327352832 | bytes 8388608 | tf_op jit(solution)/shard_map/pallas_call | solution.py:385
  64.3 1.0 %copy.9 = bf16[1,1,256,8,256]{4,3,2,1,0:T(8,128)(2,1)} copy(bf16[1,1,256,8,256]{4,3,2,1,0:T(8,128)(2,1)S(1)} %bitcast.6) | data formatting | bytes 2097152

commit v4 on v3

--- a/solution.py
+++ b/solution.py
@@ -121,13 +121,13 @@
 
     load_left = pltpu.make_async_copy(left_hbm, raw.at[0], load_sem.at[0])
     load_right = pltpu.make_async_copy(right_hbm, raw.at[1], load_sem.at[1])
+    load_tensor = pltpu.make_async_copy(tensor_hbm, tensor_ref, load_sem.at[2])
+    load_tensor.start()
     load_left.start()
     load_right.start()
-    load_tensor = pltpu.make_async_copy(tensor_hbm, tensor_ref, load_sem.at[2])
-    load_tensor.start()
 
     def load_initial(i):
-        span = pl.ds(i * 2 * part, 2 * part)
+        span = pl.ds(i * 4 * part, 4 * part)
         return pltpu.make_async_copy(initial_hbm.at[:, span, :], initial_v.at[:, span, :], initial_sem.at[i])
 
     load_initial(0).start()
@@ -148,6 +148,9 @@
         pl.semaphore_signal(barrier, inc=1, device_id=(rows - 1, far_col), device_id_type=MESH)
 
     kept = kept_ref[0, 0]
+    load_tensor.wait()
+    operator[...] = block_operator(tensor_ref, charges_ref, inner, group).astype(BF16)
+
     load_left.wait()
     load_initial(1).start()
     to, frm = iota((full, full), 0), iota((full, full), 1)
@@ -219,9 +222,6 @@
             @pl.when(jnp.logical_not(crosses))
             def _():
                 boundary_copy(step, 1, i).start()
-
-    load_tensor.wait()
-    operator[...] = block_operator(tensor_ref, charges_ref, inner, group).astype(BF16)
 
     load_right.wait()
     split = jnp.where(frm == (to % keys) * inner + to // keys, 1.0, 0.0).astype(BF16)
@@ -264,57 +264,69 @@
     def choose(i, carry):
         load_initial(i).wait()
 
-        @pl.when(i < CHUNKS // 2 - 2)
-        def _():
-            load_initial(i + 2).start()
-
-        at = pl.multiple_of(i * 2 * part, 2 * part)
-        span = pl.ds(at, 2 * part)
-        x = initial_v[0, span, :] * jnp.full((2 * part, outer), flags[0], F32).astype(BF16)
+        at = pl.multiple_of(i * 4 * part, 4 * part)
+        span = pl.ds(at, 4 * part)
+        x = initial_v[0, span, :] * jnp.full((4 * part, outer), flags[0], F32).astype(BF16)
         for e in range(1, envs):
-            x = x + initial_v[e, span, :] * jnp.full((2 * part, outer), flags[e], F32).astype(BF16)
+            x = x + initial_v[e, span, :] * jnp.full((4 * part, outer), flags[e], F32).astype(BF16)
         chosen[span, :] = x
         absorb_sites(x, 0, at)
         return carry
 
-    lax.fori_loop(0, CHUNKS // 2, choose, 0)
-
-    def give_first(h):
+    lax.fori_loop(0, CHUNKS // 4, choose, 0)
+
+    def give_first(h, lo=0, hi=CHUNKS):
+        span = pl.ds(lo * keys, (hi - lo) * keys)
         for p in range(pairs):
-            acc[h, p] = dot(left_in[...], sites[h, p])
-        for i in range(CHUNKS):
+            acc[h, p, span, :] = dot(left_in[span, :], sites[h, p])
+        for i in range(lo, hi):
             outgoing[0, h, i * part : (i + 1) * part, :] = merged((h,), i)
 
             @pl.when(working(0))
             def _(i=i):
                 give(0, h, i)
 
+    def second(i, carry):
+        at = pl.multiple_of(i * 4 * part, 4 * part)
+        absorb_sites(chosen[pl.ds(at, 4 * part), :], 1, at)
+        return carry
+
+    late = lax.rem(col, cols // 2) == 0
+
+    @pl.when(odd)
+    def _():
+        for i in range(LEFT_PARTS):
+            left_copy(i).wait_recv()
+        give_first(0)
+        lax.fori_loop(0, CHUNKS // 4, second, 0)
+        give_first(1)
+
+    @pl.when(jnp.logical_not(odd))
+    def _():
+        lax.fori_loop(0, CHUNKS // 4, second, 0)
+
+    @pl.when(jnp.logical_not(odd | late))
+    def _():
+        for i in range(LEFT_PARTS):
+            left_copy(i).wait_recv()
+        for h in range(2):
+            give_first(h)
+
+    @pl.when(late)
+    def _():
+        for n in range(2):
+            for i in range(LEFT_PARTS // 2):
+                left_copy(n * LEFT_PARTS // 2 + i).wait_recv()
+            for h in range(2):
+                give_first(h, n * CHUNKS // 2, (n + 1) * CHUNKS // 2)
+
     @pl.when(relays)
     def _():
         for i in range(CHUNKS):
             pass_on(0, i)
 
-    def second(i, carry):
-        at = pl.multiple_of(i * 2 * part, 2 * part)
-        absorb_sites(chosen[pl.ds(at, 2 * part), :], 1, at)
-        return carry
-
-    @pl.when(jnp.logical_not(odd))
-    def _():
-        lax.fori_loop(0, CHUNKS // 2, second, 0)
-
-    for i in range(LEFT_PARTS):
-        left_copy(i).wait_recv()
-    give_first(0)
-
-    @pl.when(odd)
-    def _():
-        lax.fori_loop(0, CHUNKS // 2, second, 0)
-
-    give_first(1)
-
     def later(step):
-        def take(i, carry, count=2):
+        def take(i, carry, count=2, last=False):
             for n in range(count):
                 for h in range(2):
                     boundary_copy(step - 1, h, i * count + n).wait_recv()
@@ -326,7 +338,12 @@
                 absorb_sites(x, h, at)
             for h in range(2):
                 for p in range(pairs):
-                    acc[h, p] += dot(left_in[:, span], sites[h, p, span, :])
+                    total = acc[h, p] + dot(left_in[:, span], sites[h, p, span, :])
+                    if last:
+                        for n in range(2):
+                            out_ref[2 * p + n, :, h * lanes : (h + 1) * lanes] = total[:, n * lanes : (n + 1) * lanes].astype(BF16)
+                    else:
+                        acc[h, p] = total
             return carry
 
         if step == ABSORB - 1:
@@ -338,16 +355,18 @@
 
         acc[...] = jnp.zeros_like(acc)
         lax.fori_loop(0, CHUNKS // 2 - 1, take, 0)
-        lax.fori_loop(CHUNKS - 2, CHUNKS, functools.partial(take, count=1), 0)
+        if step < ABSORB - 1:
+            lax.fori_loop(CHUNKS - 2, CHUNKS, functools.partial(take, count=1), 0)
+        else:
+            lax.fori_loop(CHUNKS - 2, CHUNKS - 1, functools.partial(take, count=1), 0)
+            take(CHUNKS - 1, 0, count=1, last=True)
+            return
 
         for i in range(CHUNKS):
             made = merged((0, 1), i)
-            if step < ABSORB - 1:
-                for h in range(2):
-                    outgoing[step, h, i * part : (i + 1) * part, :] = made[:, h * lanes : (h + 1) * lanes]
-                    give(step, h, i)
-            else:
-                out_ref[i * part : (i + 1) * part, :] = made
+            for h in range(2):
+                outgoing[step, h, i * part : (i + 1) * part, :] = made[:, h * lanes : (h + 1) * lanes]
+                give(step, h, i)
 
     for step in range(1, ABSORB):
 
@@ -384,7 +403,7 @@
     hbm = pl.BlockSpec(memory_space=pltpu.HBM)
     out = pl.pallas_call(
         functools.partial(kernel, outer, inner, envs),
-        out_shape=pltpu.VMEM((size, outer), BF16),
+        out_shape=pltpu.VMEM((inner, outer, outer), BF16),
         in_specs=[smem, smem, smem, hbm, hbm, hbm, hbm],
         out_specs=vmem,
         scratch_shapes=[
@@ -395,14 +414,14 @@
             pltpu.VMEM((2, inner // 2, outer, outer), BF16),
             pltpu.VMEM((outer, size), BF16),
             pltpu.VMEM((outer, size), BF16),
-            pltpu.VMEM((2, inner, 2 * size // CHUNKS, outer // 2), BF16),
+            pltpu.VMEM((2, inner, 4 * size // CHUNKS, outer // 2), BF16),
             pltpu.VMEM((2, inner // 2, size, outer), BF16),
             pltpu.VMEM((2, inner // 2, outer, outer), F32),
             pltpu.VMEM((outer, outer), BF16),
             pltpu.VMEM((ABSORB - 1, 2, size, outer // 2), BF16),
             pltpu.VMEM((ABSORB - 1, 2, size, outer // 2), BF16),
             pltpu.SemaphoreType.DMA((3,)),
-            pltpu.SemaphoreType.DMA((CHUNKS // 2,)),
+            pltpu.SemaphoreType.DMA((CHUNKS // 4,)),
             pltpu.SemaphoreType.DMA((LEFT_PARTS,)),
             pltpu.SemaphoreType.DMA((LEFT_PARTS,)),
             pltpu.SemaphoreType.DMA((ABSORB - 1, 2, CHUNKS)),
@@ -426,7 +445,7 @@
         right_proj.reshape(size, outer),
         left_proj.reshape(size, outer),
     )
-    return out.reshape(1, 1, outer, inner, outer)
+    return out.transpose(1, 0, 2)[None, None]
 
 
 def solution(mesh):

time: 65.4 us -> 62.8 us (0.960)
  the two profiles are of different devices: /device:TPU:16 before, /device:TPU:48 now
where the time goes in v4:
time: 62.8 us; the launch traced here: 62.6 us
  Pallas kernels  60.4 us (96%)
  local copies, waits for them, and re-layouts  1.55 us (2%)
  between operations  0.66 us (1%)
    pallas_call x1, Pallas kernels, shards(): pl.pallas_call(functools.partial(kernel, outer, inner, envs), out_shape=p...  60.4 us
    broadcast_in_dim x1, local copies, waits for them, and re-layouts, shards(): return out.transpose(1, 0, 2)[None, None]  1.55 us

profile of v4, /device:TPU:48, one launch (start us, length us, event | category | flops | bytes accessed | tf_op | source)
XLA Modules:
  0.0 62.6 jit_solution(15518667734479114460)
XLA Ops:
  0.7 60.4 %shard_map.73 = bf16[8,256,256]{2,1,0:T(8,128)(2,1)S(1)} custom-call(s32[4]{0:T(128)} %start_ref.1, s32[1,1]{1,0:T(1,128)S(6)} %copy.9.kept_ref, s32[4,8]{1,0:T(4,128)} %bitcast.13, bf16[1,4096]{1,0:T(2,128)(2,1)} %bitcast.12, bf16[4,2048,256]{2,1,0:T(8,128)(2,1)} %bitcast.9, bf16[2048,256]{1,0:T(8,128)(2,1)} %bitcast.10, bf16[2048,256]{1,0:T(8,128)(2,1)} %bitcast.11), custom_call_target="tpu_custom_call" | custom-call | flops 19327352832 | bytes 8388608 | tf_op jit(solution)/shard_map/pallas_call | solution.py:404
  61.0 1.6 %copy.8 = bf16[1,1,256,8,256]{4,3,2,1,0:T(8,128)(2,1)} copy(bf16[1,1,256,8,256]{4,2,3,1,0:T(8,128)(2,1)S(1)} %bitcast.8) | data formatting | bytes 2097152 | tf_op jit(solution)/shard_map/broadcast_in_dim | solution.py:448

commit v5 on v4

--- a/solution.py
+++ b/solution.py
@@ -93,6 +93,7 @@
     passing,
     relay_send,
     relay_recv,
+    turn,
 ):
     rows, cols = lax.axis_size("row"), lax.axis_size("col")
     row, col = lax.axis_index("row"), lax.axis_index("col")
@@ -110,10 +111,13 @@
     def working(step):
         return (row >= step) & (row <= rows - ABSORB + step)
 
-    cross = rows // 2 - 1
-    crosses = row == cross
-    relays = row == rows - 1
+    turn_rows = rows // 2
+    cross = turn_rows - 1
     lands = row == cross + 1
+    crosses = (row == cross) | lands
+    relays = (row == rows - 1) | (row == 0)
+    behind_relay = (row == cross + 1) | (row == cross + 2)
+    opposite = lax.rem(row + turn_rows, rows)
     far_col = lax.rem(col + cols // 2, cols)
     sends_any = row < rows - 1
     receives_any = row > 0
@@ -141,11 +145,12 @@
 
     @pl.when(relays)
     def _():
-        pl.semaphore_signal(barrier, inc=1, device_id=(cross, far_col), device_id_type=MESH)
-
-    @pl.when(lands)
-    def _():
-        pl.semaphore_signal(barrier, inc=1, device_id=(rows - 1, far_col), device_id_type=MESH)
+        pl.semaphore_signal(barrier, inc=1, device_id=(opposite, far_col), device_id_type=MESH)
+
+    @pl.when(behind_relay)
+    def _():
+        before = lax.rem(row + turn_rows - 1, rows)
+        pl.semaphore_signal(barrier, inc=1, device_id=(before, far_col), device_id_type=MESH)
 
     kept = kept_ref[0, 0]
     load_tensor.wait()
@@ -191,7 +196,7 @@
             dst_ref=passing.at[step, span, :],
             send_sem=send_sem.at[step, 1, i],
             recv_sem=relay_recv.at[step, i],
-            device_id=(rows - 1, far_col),
+            device_id=(opposite, far_col),
             device_id_type=MESH,
         )
 
@@ -202,24 +207,30 @@
             dst_ref=arrived.at[step, 1, span, :],
             send_sem=relay_send.at[step, i],
             recv_sem=recv_sem.at[step, 1, i],
-            device_id=(cross + 1, far_col),
+            device_id=(lax.rem(row + turn_rows + 1, rows), far_col),
             device_id_type=MESH,
         )
 
     def pass_on(step, i):
         to_relay(step, i).wait_recv()
         from_relay(step, i).start()
+
+    def relayed(step):
+        shared = lax.rem(col, cols // 2) < 2
+        main = (row == cross) | (row == rows - 1)
+        return main | shared if step > 0 else main & shared
 
     def give(step, h, i):
         if h == 0:
             boundary_copy(step, 0, i).start()
         else:
-
-            @pl.when(crosses)
+            around = crosses & relayed(step)
+
+            @pl.when(around)
             def _():
                 to_relay(step, i).start()
 
-            @pl.when(jnp.logical_not(crosses))
+            @pl.when(jnp.logical_not(around))
             def _():
                 boundary_copy(step, 1, i).start()
 
@@ -320,16 +331,28 @@
             for h in range(2):
                 give_first(h, n * CHUNKS // 2, (n + 1) * CHUNKS // 2)
 
-    @pl.when(relays)
+    @pl.when(relays & relayed(0))
     def _():
         for i in range(CHUNKS):
             pass_on(0, i)
+
+    @pl.when(relays & relayed(1))
+    def _():
+        for i in range(CHUNKS):
+            pass_on(1, i)
+
+    in_turn = jnp.logical_not(lands)
 
     def later(step):
         def take(i, carry, count=2, last=False):
             for n in range(count):
                 for h in range(2):
                     boundary_copy(step - 1, h, i * count + n).wait_recv()
+
+            if step < ABSORB - 1 and count == 2:
+                @pl.when(in_turn & jnp.logical_not(odd) & (i == 1))
+                def _():
+                    pl.semaphore_signal(turn, inc=1, device_id=(row, right_col), device_id_type=MESH)
 
             at = pl.multiple_of(i * count * part, count * part)
             span = pl.ds(at, count * part)
@@ -346,13 +369,6 @@
                         acc[h, p] = total
             return carry
 
-        if step == ABSORB - 1:
-
-            @pl.when(relays)
-            def _():
-                for i in range(CHUNKS):
-                    pass_on(step - 1, i)
-
         acc[...] = jnp.zeros_like(acc)
         lax.fori_loop(0, CHUNKS // 2 - 1, take, 0)
         if step < ABSORB - 1:
@@ -362,6 +378,10 @@
             take(CHUNKS - 1, 0, count=1, last=True)
             return
 
+        @pl.when(in_turn & odd)
+        def _():
+            pl.semaphore_wait(turn, 1)
+
         for i in range(CHUNKS):
             made = merged((0, 1), i)
             for h in range(2):
@@ -389,7 +409,7 @@
                 for i in range(CHUNKS):
                     boundary_copy(step, h, i).wait_send()
 
-        @pl.when(relays)
+        @pl.when(relays & relayed(step))
         def _(step=step):
             for i in range(CHUNKS):
                 from_relay(step, i).wait_send()
@@ -429,6 +449,7 @@
             pltpu.VMEM((ABSORB - 1, size, outer // 2), BF16),
             pltpu.SemaphoreType.DMA((ABSORB - 1, CHUNKS)),
             pltpu.SemaphoreType.DMA((ABSORB - 1, CHUNKS)),
+            pltpu.SemaphoreType.REGULAR,
         ],
         compiler_params=pltpu.CompilerParams(
             collective_id=0, has_side_effects=True, vmem_limit_bytes=58 * 1024 * 1024

time: 62.8 us -> 61 us (0.971)
  the two profiles are of different devices: /device:TPU:48 before, /device:TPU:16 now
where the time goes in v5:
time: 61 us; the launch traced here: 60.2 us
  Pallas kernels  57.9 us (95%)
  local copies, waits for them, and re-layouts  1.55 us (3%)
  between operations  0.66 us (1%)
    pallas_call x1, Pallas kernels, shards(): pl.pallas_call(functools.partial(kernel, outer, inner, envs), out_shape=p...  57.9 us
    broadcast_in_dim x1, local copies, waits for them, and re-layouts, shards(): return out.transpose(1, 0, 2)[None, None]  1.55 us

profile of v5, /device:TPU:16, one launch (start us, length us, event | category | flops | bytes accessed | tf_op | source)
XLA Modules:
  0.0 60.2 jit_solution(2810328896779287759)
XLA Ops:
  0.7 57.9 %shard_map.73 = bf16[8,256,256]{2,1,0:T(8,128)(2,1)S(1)} custom-call(s32[4]{0:T(128)} %start_ref.1, s32[1,1]{1,0:T(1,128)S(6)} %copy.9.kept_ref, s32[4,8]{1,0:T(4,128)} %bitcast.13, bf16[1,4096]{1,0:T(2,128)(2,1)} %bitcast.12, bf16[4,2048,256]{2,1,0:T(8,128)(2,1)} %bitcast.9, bf16[2048,256]{1,0:T(8,128)(2,1)} %bitcast.10, bf16[2048,256]{1,0:T(8,128)(2,1)} %bitcast.11), custom_call_target="tpu_custom_call" | custom-call | flops 19327352832 | bytes 8388608 | tf_op jit(solution)/shard_map/pallas_call | solution.py:424
  58.6 1.6 %copy.8 = bf16[1,1,256,8,256]{4,3,2,1,0:T(8,128)(2,1)} copy(bf16[1,1,256,8,256]{4,2,3,1,0:T(8,128)(2,1)S(1)} %bitcast.8) | data formatting | bytes 2097152 | tf_op jit(solution)/shard_map/broadcast_in_dim | solution.py:469

commit v6 on v5

--- a/solution.py
+++ b/solution.py
@@ -370,11 +370,12 @@
             return carry
 
         acc[...] = jnp.zeros_like(acc)
-        lax.fori_loop(0, CHUNKS // 2 - 1, take, 0)
         if step < ABSORB - 1:
+            lax.fori_loop(0, CHUNKS // 2 - 1, take, 0)
             lax.fori_loop(CHUNKS - 2, CHUNKS, functools.partial(take, count=1), 0)
         else:
-            lax.fori_loop(CHUNKS - 2, CHUNKS - 1, functools.partial(take, count=1), 0)
+            lax.fori_loop(0, CHUNKS // 2 - 2, take, 0)
+            lax.fori_loop(CHUNKS - 4, CHUNKS - 1, functools.partial(take, count=1), 0)
             take(CHUNKS - 1, 0, count=1, last=True)
             return
 

time: 61 us -> 62 us (1.016)
  Pallas kernels: 57.9 us -> 58.9 us
    pallas_call x1, Pallas kernels: 57.9 us -> 58.9 us  [shards(): pl.pallas_call(functools.partial(kernel, outer, inner, envs), out_shape=p...]
where the time goes in v6:
time: 62 us; the launch traced here: 61.1 us
  Pallas kernels  58.9 us (95%)
  local copies, waits for them, and re-layouts  1.55 us (2%)
  between operations  0.66 us (1%)
    pallas_call x1, Pallas kernels, shards(): pl.pallas_call(functools.partial(kernel, outer, inner, envs), out_shape=p...  58.9 us
    broadcast_in_dim x1, local copies, waits for them, and re-layouts, shards(): return out.transpose(1, 0, 2)[None, None]  1.55 us

profile of v6, /device:TPU:16, one launch (start us, length us, event | category | flops | bytes accessed | tf_op | source)
XLA Modules:
  0.0 61.1 jit_solution(10487170319505688644)
XLA Ops:
  0.7 58.9 %shard_map.73 = bf16[8,256,256]{2,1,0:T(8,128)(2,1)S(1)} custom-call(s32[4]{0:T(128)} %start_ref.1, s32[1,1]{1,0:T(1,128)S(6)} %copy.9.kept_ref, s32[4,8]{1,0:T(4,128)} %bitcast.13, bf16[1,4096]{1,0:T(2,128)(2,1)} %bitcast.12, bf16[4,2048,256]{2,1,0:T(8,128)(2,1)} %bitcast.9, bf16[2048,256]{1,0:T(8,128)(2,1)} %bitcast.10, bf16[2048,256]{1,0:T(8,128)(2,1)} %bitcast.11), custom_call_target="tpu_custom_call" | custom-call | flops 19327352832 | bytes 8388608 | tf_op jit(solution)/shard_map/pallas_call | solution.py:425
  59.5 1.6 %copy.8 = bf16[1,1,256,8,256]{4,3,2,1,0:T(8,128)(2,1)} copy(bf16[1,1,256,8,256]{4,2,3,1,0:T(8,128)(2,1)S(1)} %bitcast.8) | data formatting | bytes 2097152 | tf_op jit(solution)/shard_map/broadcast_in_dim | solution.py:470

commit v7 on v5

--- a/solution.py
+++ b/solution.py
@@ -374,8 +374,7 @@
         if step < ABSORB - 1:
             lax.fori_loop(CHUNKS - 2, CHUNKS, functools.partial(take, count=1), 0)
         else:
-            lax.fori_loop(CHUNKS - 2, CHUNKS - 1, functools.partial(take, count=1), 0)
-            take(CHUNKS - 1, 0, count=1, last=True)
+            take(CHUNKS // 2 - 1, 0, last=True)
             return
 
         @pl.when(in_turn & odd)

time: 61 us -> 60.5 us (level)
  no operation moved by 1% of the time
where the time goes in v7:
time: 60.5 us; the launch traced here: 59.6 us
  Pallas kernels  57.3 us (95%)
  local copies, waits for them, and re-layouts  1.55 us (3%)
  between operations  0.66 us (1%)
    pallas_call x1, Pallas kernels, shards(): pl.pallas_call(functools.partial(kernel, outer, inner, envs), out_shape=p...  57.3 us
    broadcast_in_dim x1, local copies, waits for them, and re-layouts, shards(): return out.transpose(1, 0, 2)[None, None]  1.55 us

profile of v7, /device:TPU:16, one launch (start us, length us, event | category | flops | bytes accessed | tf_op | source)
XLA Modules:
  0.0 59.6 jit_solution(6255369302043795614)
XLA Ops:
  0.7 57.3 %shard_map.73 = bf16[8,256,256]{2,1,0:T(8,128)(2,1)S(1)} custom-call(s32[4]{0:T(128)} %start_ref.1, s32[1,1]{1,0:T(1,128)S(6)} %copy.9.kept_ref, s32[4,8]{1,0:T(4,128)} %bitcast.13, bf16[1,4096]{1,0:T(2,128)(2,1)} %bitcast.12, bf16[4,2048,256]{2,1,0:T(8,128)(2,1)} %bitcast.9, bf16[2048,256]{1,0:T(8,128)(2,1)} %bitcast.10, bf16[2048,256]{1,0:T(8,128)(2,1)} %bitcast.11), custom_call_target="tpu_custom_call" | custom-call | flops 19327352832 | bytes 8388608 | tf_op jit(solution)/shard_map/pallas_call | solution.py:423
  58.0 1.6 %copy.8 = bf16[1,1,256,8,256]{4,3,2,1,0:T(8,128)(2,1)} copy(bf16[1,1,256,8,256]{4,2,3,1,0:T(8,128)(2,1)S(1)} %bitcast.8) | data formatting | bytes 2097152 | tf_op jit(solution)/shard_map/broadcast_in_dim | solution.py:468
